TPU v7x, 32 devices: a whole 2x2x4 slice. The times are simulated.
32 devices in a mesh: groups: 2 (over y), dp: 4 (over z), mp: 4 (over x, core).
Axes of the slice: x: 2, y: 2, z: 4, core: 2. Of those that a mesh axis runs over, the one named last changes fastest.
Arguments:
- layer_input: bfloat16 [8192, 4096], P(('groups', 'dp'), 'mp'), parts along dimension 0, may hold values from -6 to 6
- output_grad: bfloat16 [8192, 4096], P(('groups', 'dp'), 'mp'), parts along dimension 0, may hold values from -6 to 6
- gate_preact: bfloat16 [8192, 11008], P(('groups', 'dp'), 'mp'), parts along dimension 0, may hold values from -6 to 6
- up_values: bfloat16 [8192, 11008], P(('groups', 'dp'), 'mp'), parts along dimension 0, may hold values from -6 to 6
- down_weight: bfloat16 [11008, 4096], P('mp', 'dp'), may hold values from -0.09375 to 0.09375
- up_in_factor: bfloat16 [4096, 64], P('mp'), may hold values from -0.09375 to 0.09375
- up_out_factor: bfloat16 [11008, 64], P('mp'), may hold values from -0.0546875 to 0.0546875
- down_in_factor: bfloat16 [11008, 64], P('mp'), may hold values from -0.0546875 to 0.0546875
- down_out_factor: bfloat16 [4096, 64], P('mp'), may hold values from -0.09375 to 0.09375
- queries: bfloat16 [64, 8192], P(('groups', 'dp')), parts along dimension 0, may hold values from -0.005859375 to 0.005859375
Outputs:
- scores: float32 [32, 32], P(('groups', 'dp')), parts along dimension 0
There are 2 independent parts, one for each index of `groups`. A program takes and returns all parts, laid end to end along the dimension named above; an argument that names none is the same for every part. Nothing has to cross between parts.
All inputs are finite; a program needn't handle non-finite values.
Results may differ from a plain program's by a relative error of at most 0.0042.
Values may be sent and summed in bfloat16 or wider, within the bound.
A program may use at most 128 MiB of HBM per device.

v0:
```python
import jax
import jax.numpy as jnp
from jax import lax
from jax.sharding import PartitionSpec as P

SEQ = 256


def outer_sums(first, second):
    return jnp.einsum("nti,ntj->nij", first, second, precision=lax.Precision.HIGHEST)


def body(
    layer_input,
    output_grad,
    gate_preact,
    up_values,
    down_weight,
    up_in_factor,
    up_out_factor,
    down_in_factor,
    down_out_factor,
    queries,
):
    grad_full = lax.all_gather(output_grad, "mp", axis=1, tiled=True)
    row_count = output_grad.shape[0]
    rank_dim = up_in_factor.shape[1]
    examples_here = row_count // SEQ
    back = lax.dot_general(
        grad_full,
        lax.all_gather(down_weight, "dp", axis=1, tiled=True),
        (((1,), (1,)), ((), ())),
        preferred_element_type=jnp.float32,
    )
    silu_gate = jax.nn.silu(gate_preact.astype(jnp.float32))
    hidden = (silu_gate * up_values.astype(jnp.float32)).astype(jnp.bfloat16)
    up_grad = (back * silu_gate).astype(jnp.bfloat16)
    partial_value = jnp.concatenate(
        [
            jnp.dot(layer_input, up_in_factor, preferred_element_type=jnp.float32),
            jnp.dot(up_grad, up_out_factor, preferred_element_type=jnp.float32),
            jnp.dot(hidden, down_in_factor, preferred_element_type=jnp.float32),
            jnp.dot(output_grad, down_out_factor, preferred_element_type=jnp.float32),
        ],
        1,
    )
    summed = lax.psum(partial_value, "mp").reshape(examples_here, SEQ, 4 * rank_dim)
    sketch_up = outer_sums(summed[:, :, :rank_dim], summed[:, :, rank_dim : 2 * rank_dim])
    sketch_down = outer_sums(
        summed[:, :, 2 * rank_dim : 3 * rank_dim], summed[:, :, 3 * rank_dim :]
    )
    sketch_part = jnp.concatenate(
        [
            sketch_up.reshape(examples_here, rank_dim * rank_dim),
            sketch_down.reshape(examples_here, rank_dim * rank_dim),
        ],
        1,
    )
    sketch_low = sketch_part.astype(jnp.bfloat16)
    return lax.dot_general(
        sketch_low,
        lax.all_gather(queries, "dp", axis=0, tiled=True),
        (((1,), (1,)), ((), ())),
        preferred_element_type=jnp.float32,
    )


def solution(mesh):
    return jax.shard_map(
        body,
        mesh=mesh,
        in_specs=(
            P(("groups", "dp"), "mp"),
            P(("groups", "dp"), "mp"),
            P(("groups", "dp"), "mp"),
            P(("groups", "dp"), "mp"),
            P("mp", "dp"),
            P("mp", None),
            P("mp", None),
            P("mp", None),
            P("mp", None),
            P(("groups", "dp"), None),
        ),
        out_specs=P(("groups", "dp"), None),
        check_vma=False,
    )
```

profile of v0, /device:TPU:0, one launch (start us, length us, event | category | flops | bytes accessed | tf_op | source)
XLA Modules:
  0.0 534.6 jit_solution(14972066526075621979)
XLA Ops:
  6.5 0.0 copy-start
  6.5 0.0 copy-start.1
  6.5 0.0 copy-start.3
  6.5 0.0 all-gather.3.cloned.1.call-start
  6.5 0.7 all-gather.3.cloned.1.call-update
  7.3 0.0 all-gather.5.cloned.1.call-start
  7.3 0.7 all-gather.5.cloned.1.call-update
  8.0 0.0 all-reduce.2.cloned.1.call-start
  8.1 2.4 fusion.17
  10.4 0.0 copy-done
  10.4 0.0 copy-done.1
  10.4 0.8 fusion.16
  11.2 0.0 copy-done.3
  11.2 6.3 %fusion.3 = f32[1024,64]{0,1:T(8,128)S(1)} fusion(bf16[2752,64]{0,1:T(8,128)(2,1)S(1)} %copy-done.3, bf16[1024,2752]{0,1:T(8,128)(2,1)} %param.13, bf16[1024,2752]{0,1:T(8,128)(2,1)} %param.12), kind=kOutput, calls=%fused_computation.7 | convolution fusion | flops 383254528 | bytes 11886592 | tf_op jit(solution)/shard_map/dot_general | solution.py:42
  17.5 0.0 copy-start.2
  17.5 52.5 %all-gather.3.cloned.1.call-done = bf16[1024,4096]{1,0:T(8,128)(2,1)} async-done(((bf16[1024,1024]{1,0:T(8,128)(2,1)}), bf16[1024,4096]{1,0:T(8,128)(2,1)}) %all-gather.3.cloned.1.call-update) | async-done | bytes 8388624 | tf_op jit(solution)/shard_map/all_gather | solution.py:25
  69.9 384.1 %all-gather.5.cloned.1.call-done = bf16[2752,4096]{1,0:T(8,128)(2,1)} async-done(((bf16[2752,1024]{1,0:T(8,128)(2,1)}), bf16[2752,4096]{1,0:T(8,128)(2,1)}) %all-gather.5.cloned.1.call-update) | async-done | bytes 22544400 | tf_op jit(solution)/shard_map/all_gather | solution.py:31
  454.1 34.3 %fusion.4 = f32[1024,64]{0,1:T(8,128)S(1)} fusion(bf16[2752,64]{0,1:T(8,128)(2,1)} %param.16, bf16[1024,4096]{1,0:T(8,128)(2,1)} %all-gather.3.cloned.1.call-done, bf16[2752,4096]{1,0:T(8,128)(2,1)} %all-gather.5.cloned.1.call-done, bf16[1024,2752]{0,1:T(8,128)(2,1)} %param.12), kind=kOutput, calls=%fused_computation.8 | convolution fusion | flops 23465885696 | bytes 37183488 | tf_op jit(solution)/shard_map/dot_general | solution.py:41
  488.4 0.1 pad_maximum_fusion
  488.5 1.1 copy.14
  489.6 0.0 all-reduce.2.cloned.1.call-update
  489.6 0.0 copy-done.2
  489.6 16.2 %all_gather.11 = bf16[32,8192]{1,0:T(8,128)(2,1)S(1)} all-gather(bf16[8,8192]{1,0:T(8,128)(2,1)S(1)} %copy-done.2), channel_id=1, replica_groups=mesh['groups'=2,'dp'=4,'mp'=4] {'dp'}, dimensions={0}, use_global_device_ids=true | all-gather | bytes 655360 | tf_op jit(solution)/shard_map/all_gather | solution.py:62
  505.8 18.4 %all-reduce.2.cloned.1.call-done = f32[4,256,256]{1,2,0:T(8,128)} async-done(((f32[4,256,256]{1,2,0:T(8,128)}), f32[4,256,256]{1,2,0:T(8,128)}) %all-reduce.2.cloned.1.call-update) | async-done | bytes 1048592 | tf_op jit(solution)/shard_map/psum | solution.py:47
  524.2 1.4 convolution_convert_fusion
  525.6 0.1 reshape.13
  525.7 1.4 convolution_convert_fusion.1
  527.2 0.1 reshape.12
  527.3 0.8 fusion.9
Async XLA Ops:
  6.5 3.9 copy-start
  6.5 3.9 copy-start.1
  6.5 4.7 copy-start.3
  6.5 63.4 %all-gather.3.cloned.1.call-start = ((), (), s32[]{:S(2)}) async-start(), calls=%async_computation | async-start | bytes 10485760 | tf_op jit(solution)/shard_map/all_gather | solution.py:25
  7.3 446.8 %all-gather.5.cloned.1.call-start = ((), (), s32[]{:S(2)}) async-start(), calls=%async_computation.1 | async-start | bytes 28180480 | tf_op jit(solution)/shard_map/all_gather | solution.py:31
  8.0 516.2 %all-reduce.2.cloned.1.call-start = ((), (), s32[]{:S(2)}) async-start(), calls=%async_computation.2 | async-start | bytes 2097152 | tf_op jit(solution)/shard_map/psum | solution.py:47
  17.5 472.2 %copy-start.2 = (bf16[8,8192]{1,0:T(8,128)(2,1)S(1)}, bf16[8,8192]{1,0:T(8,128)(2,1)}, u32[]{:S(2)}) copy-start(bf16[8,8192]{1,0:T(8,128)(2,1)} %param.19) | copy-start | bytes 393220
Sparse Core Ops, SparseCore 0:
  8.9 60.9 all-gather.2
  71.5 382.5 all-gather.4
  489.7 34.4 all-reduce.1
where the time goes:
time: 535 us
  waiting for transfers between devices  456 us (85%)
  matrix products  47.3 us (9%)
  blocking collectives  16.2 us (3%)
  between operations  13.2 us (2%)
    all_gather x1, waiting for transfers between devices, body(): lax.all_gather(down_weight, 'dp', axis=1, tiled=True)  384 us
    all_gather x1, waiting for transfers between devices, body(): grad_full = lax.all_gather(output_grad, 'mp', axis=1, tiled=True)  52.5 us
    dot_general x1, matrix products, body(): jnp.dot(up_grad, up_out_factor, preferred_element_type=jnp.float32)  34.3 us
    psum x1, waiting for transfers between devices, body(): lax.psum(partial_value, 'mp').reshape(examples_here, SEQ, 4 * rank_dim)  18.4 us
    all_gather x1, blocking collectives, body(): lax.all_gather(queries, 'dp', axis=0, tiled=True)  16.2 us
  transfers between devices with their start and end apart: 3, of which 3 were waited for; matrix products, arithmetic and copies ran while one was open for 2% of the time, Pallas kernels for 0%

commit v1 on v0

v1 whole, which is shorter than its diff:
```python
import functools

import jax
import jax.numpy as jnp
from jax import lax
from jax.experimental import pallas as pl
from jax.experimental.pallas import tpu as pltpu
from jax.sharding import PartitionSpec as P

SEQ = 256
PIECES = 4
MESH = pl.DeviceIdType.MESH
NT = (((1,), (1,)), ((), ()))


def cuts(total, parts):
    units = -(-total // 128)
    parts = min(parts, units)
    edges = [min(total, 128 * ((units * i + parts - 1) // parts)) for i in range(parts + 1)]
    return [(a, b - a) for a, b in zip(edges[:-1], edges[1:])]


def kernel(
    sizes,
    w_ref,
    grad_ref,
    gate_ref,
    up_ref,
    up_out_ref,
    down_in_ref,
    out_up_ref,
    in_down_ref,
    wbuf,
    gbuf,
    gate,
    upbuf,
    acc,
    local_sem,
    up_sem,
    z_send,
    z_recv,
    y_send,
    y_recv,
    g_send,
    g_recv,
    r_send,
    r_recv,
):
    groups, dp, mp = sizes
    tokens = gate.shape[0]
    hidden_units, width = w_ref.shape
    half = width // groups
    gwidth = grad_ref.shape[1]
    pieces = cuts(hidden_units, PIECES)
    last = len(pieces) - 1
    y, z, m = (lax.axis_index(name) for name in ("groups", "dp", "mp"))
    x_count = mp // 2
    sibling = m + 1 - 2 * lax.rem(m, 2)
    has_lo, has_hi = z > 0, z < dp - 1
    tile = min(256, tokens)
    small = min(128, tokens)

    def x_peer(j):
        return lax.rem(m + 2 * j, mp)

    def y_peer(j):
        return lax.rem(y + j, groups)

    barrier = pltpu.get_barrier_semaphore()

    def greet(where):
        pl.semaphore_signal(barrier, inc=1, device_id=where, device_id_type=MESH)

    pl.when(has_lo)(lambda: greet({"dp": z - 1}))
    pl.when(has_hi)(lambda: greet({"dp": z + 1}))
    for j in range(1, groups):
        greet({"groups": y_peer(j)})
    greet({"mp": sibling})
    for j in range(1, x_count):
        greet({"mp": x_peer(j)})
    pl.semaphore_wait(
        barrier,
        has_lo.astype(jnp.int32) + has_hi.astype(jnp.int32) + (groups - 1) + 1 + (x_count - 1),
    )

    def w_slice(ref, c, part):
        start, size = pieces[c]
        return ref.at[pl.ds(start, size), pl.ds(pl.multiple_of(part * half, 128), half)]

    def z_block(way, k):
        return z + k if way == 0 else z - k

    def z_copy(way, k, c):
        block = z_block(way, k)
        return pltpu.make_async_remote_copy(
            src_ref=w_slice(w_ref if k == 0 else wbuf.at[block], c, y),
            dst_ref=w_slice(wbuf.at[block], c, y),
            send_sem=z_send.at[way, k, c],
            recv_sem=z_recv.at[block, c],
            device_id={"dp": z - 1 if way == 0 else z + 1},
            device_id_type=MESH,
        )

    def z_arrived(way, k, c):
        block = z_block(way, k)
        pltpu.make_async_remote_copy(
            src_ref=w_slice(wbuf.at[block], c, y),
            dst_ref=w_slice(wbuf.at[block], c, y),
            send_sem=z_send.at[way, k, c],
            recv_sem=z_recv.at[block, c],
            device_id={"groups": y_peer(1)},
            device_id_type=MESH,
        ).wait_recv()

    def y_copy(j, block, c, part):
        return pltpu.make_async_remote_copy(
            src_ref=w_slice(wbuf.at[block], c, part),
            dst_ref=w_slice(wbuf.at[block], c, part),
            send_sem=y_send.at[j - 1, block, c],
            recv_sem=y_recv.at[j - 1, block, c],
            device_id={"groups": y_peer(j)},
            device_id_type=MESH,
        )

    def valid(way, k):
        return (z + k <= dp - 1) if way == 0 else (z - k >= 0)

    def can_pass(way):
        return has_lo if way == 0 else has_hi

    def g_slice(ref, owner):
        return ref.at[:, pl.ds(pl.multiple_of(owner * gwidth, 128), gwidth)]

    def g_copy(where, owner, src, send, recv):
        return pltpu.make_async_remote_copy(
            src_ref=src,
            dst_ref=g_slice(gbuf, owner),
            send_sem=send,
            recv_sem=recv,
            device_id={"mp": where},
            device_id_type=MESH,
        )

    def g_first(j):
        where = sibling if j == 0 else x_peer(j)
        return g_copy(where, m, grad_ref, g_send.at[j], g_recv.at[j])

    def g_relay(j):
        owner = lax.rem(m + mp - 2 * j, mp)
        return g_copy(sibling, owner, g_slice(gbuf, owner), r_send.at[j - 1], r_recv.at[j - 1])

    for c in range(len(pieces)):
        for way in (0, 1):
            pl.when(can_pass(way))(lambda way=way, c=c: z_copy(way, 0, c).start())
    for j in range(1, x_count):
        g_first(j).start()
    g_first(0).start()

    gate_in = pltpu.make_async_copy(gate_ref, gate, local_sem.at[0])
    gate_in.start()
    w_in = pltpu.make_async_copy(w_ref, wbuf.at[z], local_sem.at[1])
    w_in.start()
    g_in = pltpu.make_async_copy(grad_ref, g_slice(gbuf, m), local_sem.at[2])
    g_in.start()
    gate_in.wait()
    w_in.wait()
    g_in.wait()

    def silu(rows, start, size):
        value = gate[rows, start : start + size].astype(jnp.float32)
        return value / (1.0 + jnp.exp(-value))

    def down_part(i):
        base = i * tile
        copy = pltpu.make_async_copy(up_ref.at[pl.ds(base, tile), :], upbuf, up_sem)
        copy.start()
        copy.wait()

        def step(t, _):
            inner = pl.ds(pl.multiple_of(t * small, small), small)
            rows = pl.ds(pl.multiple_of(base + t * small, small), small)
            total = jnp.zeros((small, in_down_ref.shape[1]), jnp.float32)
            for start, size in pieces:
                up = upbuf[inner, start : start + size].astype(jnp.float32)
                hidden = (silu(rows, start, size) * up).astype(jnp.bfloat16)
                total += jnp.dot(
                    hidden, down_in_ref[start : start + size, :], preferred_element_type=jnp.float32
                )
            in_down_ref[rows, :] = total
            return 0

        lax.fori_loop(0, tile // small, step, 0)

    def multiply(block, c, first):
        start, size = pieces[c]

        def step(t, _):
            rows = pl.ds(pl.multiple_of(t * tile, tile), tile)
            product = lax.dot_general(
                gbuf[rows, pl.ds(pl.multiple_of(block * width, 128), width)],
                wbuf[block, start : start + size, :],
                NT,
                preferred_element_type=jnp.float32,
            )
            if first:
                acc[rows, start : start + size] = product
            else:
                acc[rows, start : start + size] += product
            return 0

        lax.fori_loop(0, tokens // tile, step, 0)

    def finish(c):
        start, size = pieces[c]

        def step(t, _):
            rows = pl.ds(pl.multiple_of(t * small, small), small)
            up_grad = (acc[rows, start : start + size] * silu(rows, start, size)).astype(jnp.bfloat16)
            share = jnp.dot(
                up_grad, up_out_ref[start : start + size, :], preferred_element_type=jnp.float32
            )
            if c == 0:
                out_up_ref[rows, :] = share
            else:
                out_up_ref[rows, :] += share
            return 0

        lax.fori_loop(0, tokens // small, step, 0)

    def consume(k, c):
        if k == 0:
            multiply(z, c, True)
        else:
            for way in (0, 1):

                def one(way=way):
                    block = z_block(way, k)
                    for j in range(1, groups):
                        y_copy(j, block, c, lax.rem(y + groups - j, groups)).wait_recv()
                    multiply(block, c, False)

                pl.when(valid(way, k))(one)
        if k == dp - 1:
            finish(c)

    def gather_grad():
        g_first(0).wait_recv()
        for j in range(1, x_count):
            g_relay(j).wait_recv()

    down_todo = list(range(tokens // tile))
    todo = [(0, c) for c in range(len(pieces))]
    ready = False
    for k in range(1, dp):
        for c in range(len(pieces)):
            for way in (0, 1):

                def one(way=way):
                    z_arrived(way, k, c)
                    pl.when(can_pass(way))(lambda: z_copy(way, k, c).start())
                    block = z_block(way, k)
                    for j in range(1, groups):
                        y_copy(j, block, c, y).start()

                pl.when(valid(way, k))(one)
            if k == 1:
                if down_todo:
                    down_part(down_todo.pop(0))
                if c == last:
                    for j in range(1, x_count):
                        g_first(j).wait_recv()
                        g_relay(j).start()
            else:
                if not ready:
                    gather_grad()
                    ready = True
                for item in todo[:3]:
                    consume(*item)
                todo = todo[3:]
            todo.append((k, c))
    if not ready:
        gather_grad()
    while down_todo:
        down_part(down_todo.pop(0))
    for item in todo:
        consume(*item)

    for k in range(dp):
        for way in (0, 1):
            for c in range(len(pieces)):
                pl.when(valid(way, k) & can_pass(way))(
                    lambda way=way, c=c, k=k: z_copy(way, k, c).wait_send()
                )

                def sent(way=way, c=c, k=k):
                    for j in range(1, groups):
                        y_copy(j, z_block(way, k), c, y).wait_send()

                if k > 0:
                    pl.when(valid(way, k))(sent)
    for j in range(x_count):
        g_first(j).wait_send()
    for j in range(1, x_count):
        g_relay(j).wait_send()


def gather_and_project(sizes, down_weight, output_grad, gate, up, up_out, down_in):
    groups, dp, mp = sizes
    tokens, hidden_units = gate.shape
    rank = up_out.shape[1]
    width = down_weight.shape[1]
    count = len(cuts(hidden_units, PIECES))
    x_count = mp // 2
    tile = min(256, tokens)
    anywhere = pl.BlockSpec(memory_space=pl.ANY)
    vmem = pl.BlockSpec(memory_space=pltpu.VMEM)
    dma = pltpu.SemaphoreType.DMA
    part = jax.ShapeDtypeStruct((tokens, rank), jnp.float32)
    return pl.pallas_call(
        functools.partial(kernel, sizes),
        out_shape=(part, part),
        in_specs=[anywhere] * 4 + [vmem] * 2,
        out_specs=(vmem, vmem),
        scratch_shapes=[
            pltpu.VMEM((dp, hidden_units, width), jnp.bfloat16),
            pltpu.VMEM((tokens, output_grad.shape[1] * mp), jnp.bfloat16),
            pltpu.VMEM((tokens, hidden_units), jnp.bfloat16),
            pltpu.VMEM((tile, hidden_units), jnp.bfloat16),
            pltpu.VMEM((tokens, hidden_units), jnp.float32),
            dma((3,)),
            dma,
            dma((2, dp, count)),
            dma((dp, count)),
            dma((max(groups - 1, 1), dp, count)),
            dma((max(groups - 1, 1), dp, count)),
            dma((x_count,)),
            dma((x_count,)),
            dma((max(x_count - 1, 1),)),
            dma((max(x_count - 1, 1),)),
        ],
        compiler_params=pltpu.CompilerParams(
            collective_id=0, has_side_effects=True, vmem_limit_bytes=60 * 1024 * 1024
        ),
        cost_estimate=pl.CostEstimate(
            flops=2 * tokens * hidden_units * width * dp,
            bytes_accessed=4 * tokens * hidden_units,
            transcendentals=2 * tokens * hidden_units,
        ),
    )(down_weight, output_grad, gate, up, up_out, down_in)


def outer_sums(first, second):
    return jnp.einsum("nti,ntj->nij", first, second, precision=lax.Precision.HIGHEST)


def body(
    sizes,
    layer_input,
    output_grad,
    gate_preact,
    up_values,
    down_weight,
    up_in_factor,
    up_out_factor,
    down_in_factor,
    down_out_factor,
    queries,
):
    rank = up_in_factor.shape[1]
    count = output_grad.shape[0] // SEQ
    all_queries = lax.all_gather(queries, "dp", axis=0, tiled=True)
    early = lax.psum(
        jnp.concatenate(
            [
                jnp.dot(layer_input, up_in_factor, preferred_element_type=jnp.float32),
                jnp.dot(output_grad, down_out_factor, preferred_element_type=jnp.float32),
            ],
            1,
        ),
        "mp",
    ).reshape(count, SEQ, 2 * rank)
    out_up, in_down = gather_and_project(
        sizes, down_weight, output_grad, gate_preact, up_values, up_out_factor, down_in_factor
    )
    sketch = jnp.concatenate(
        [
            outer_sums(early[:, :, :rank], out_up.reshape(count, SEQ, rank)).reshape(count, -1),
            outer_sums(in_down.reshape(count, SEQ, rank), early[:, :, rank:]).reshape(count, -1),
        ],
        1,
    )
    scores = lax.dot_general(
        sketch,
        all_queries.astype(jnp.float32),
        NT,
        precision=lax.Precision.HIGHEST,
        preferred_element_type=jnp.float32,
    )
    return lax.psum(scores, "mp")


def solution(mesh):
    sizes = (mesh.shape["groups"], mesh.shape["dp"], mesh.shape["mp"])
    return jax.shard_map(
        functools.partial(body, sizes),
        mesh=mesh,
        in_specs=(
            P(("groups", "dp"), "mp"),
            P(("groups", "dp"), "mp"),
            P(("groups", "dp"), "mp"),
            P(("groups", "dp"), "mp"),
            P("mp", "dp"),
            P("mp", None),
            P("mp", None),
            P("mp", None),
            P("mp", None),
            P(("groups", "dp"), None),
        ),
        out_specs=P(("groups", "dp"), None),
        check_vma=False,
    )
```

time: 535 us -> 281 us (0.53)
  waiting for transfers between devices: 456 us -> 0.02 us
  Pallas kernels: 0 us -> 212 us
  matrix products: 47.3 us -> 7.31 us
  local copies, waits for them, and re-layouts: 1.35 us -> 20.1 us
  blocking collectives: 16.2 us -> 27.2 us
    all_gather x2 -> x0, waiting for transfers between devices: 437 us -> none  [the longest x1 384 us: body(): lax.all_gather(down_weight, 'dp', axis=1, tiled=True)]
    pallas_call x0 -> x1, Pallas kernels: none -> 212 us  [gather_and_project(): pl.pallas_call(functools.partial(kernel, sizes), out_shape=(part, part),...]
    dot_general x3 -> x1, matrix products: 41.4 us -> 0.51 us  [body(): lax.dot_general(sketch, all_queries.astype(jnp.float32), NT, precision=la...]
    unnamed x8 -> x16, local copies, waits for them, and re-layouts: 0.02 us -> 19.1 us
    psum x1, waiting for transfers between devices: 18.4 us -> 0.01 us  [body(): lax.psum(jnp.concatenate([jnp.dot(layer_input, up_in_factor, preferred_el...]
    psum x0 -> x1, blocking collectives: none -> 6.22 us  [body(): return lax.psum(scores, 'mp')]
  transfers between devices with their start and end apart: 3 -> 1, of which waited for: 3 -> 0; matrix products, arithmetic and copies ran while one was open for 2% -> 7% of each run, Pallas kernels for 0% -> 76%
where the time goes in v1:
time: 281 us; the launch traced here: 280 us
  Pallas kernels  212 us (75%)
  blocking collectives  27.2 us (10%)
  local copies, waits for them, and re-layouts  20.1 us (7%)
  between operations  13.5 us (5%)
  matrix products  7.31 us (3%)
    pallas_call x1, Pallas kernels, gather_and_project(): pl.pallas_call(functools.partial(kernel, sizes), out_shape=(part, part),...  212 us
    all_gather x1, blocking collectives, body(): all_queries = lax.all_gather(queries, 'dp', axis=0, tiled=True)  21 us
    unnamed x16, local copies, waits for them, and re-layouts  19.1 us
    psum x1, blocking collectives, body(): return lax.psum(scores, 'mp')  6.22 us
  transfers between devices with their start and end apart: 1, of which 0 were waited for; matrix products, arithmetic and copies ran while one was open for 7% of the time, Pallas kernels for 76%

profile of v1, /device:TPU:0, one launch (start us, length us, event | category | flops | bytes accessed | tf_op | source)
XLA Modules:
  0.0 280.2 jit_solution(8413653232069625151)
XLA Ops:
  6.5 0.0 copy-start
  6.5 0.0 copy-start.4
  6.5 0.0 all-reduce.2.cloned.1.call-start
  6.5 2.5 fusion.10
  9.0 0.0 copy-done
  9.0 0.0 copy-done.4
  9.1 0.8 fusion.9
  9.9 0.8 copy.22
  10.7 0.0 all-reduce.2.cloned.1.call-update
  10.7 8.3 %copy.12.gate_ref = bf16[1024,2752]{1,0:T(8,128)(2,1)} copy(bf16[1024,2752]{0,1:T(8,128)(2,1)} %param.12) | data formatting | bytes 11272192 | tf_op args[2]
  19.1 0.0 copy-start.2
  19.1 0.0 copy-start.3
  19.1 8.5 %copy.13.up_ref = bf16[1024,2752]{1,0:T(8,128)(2,1)} copy(bf16[1024,2752]{0,1:T(8,128)(2,1)} %param.13) | data formatting | bytes 11272192 | tf_op args[3]
  27.5 0.0 copy-done.2
  27.5 1.1 copy.14.up_out_ref
  28.7 0.0 copy-done.3
  28.7 1.1 copy.15.down_in_ref
  29.8 0.0 copy-start.5
  29.8 212.0 %shard_map.100 = (f32[1024,64]{1,0:T(8,128)}, f32[1024,64]{1,0:T(8,128)}) custom-call(bf16[2752,1024]{1,0:T(8,128)(2,1)} %w_ref.1, bf16[1024,1024]{1,0:T(8,128)(2,1)} %grad_ref.1, bf16[1024,2752]{1,0:T(8,128)(2,1)} %copy.12.gate_ref, bf16[1024,2752]{1,0:T(8,128)(2,1)} %copy.13.up_ref, bf16[2752,64]{1,0:T(8,128)(2,1)} %copy.14.up_out_ref, ...), custom_call_target="tpu_custom_call" | custom-call | flops 23085449216 | bytes 11272192 | tf_op jit(solution)/shard_map/pallas_call | solution.py:319
  241.8 0.0 copy-done.5
  241.8 0.0 copy-start.1
  241.8 21.0 %all_gather.3 = bf16[32,8192]{1,0:T(8,128)(2,1)S(1)} all-gather(bf16[8,8192]{1,0:T(8,128)(2,1)S(1)} %copy-done.5), channel_id=1, replica_groups=mesh['groups'=2,'dp'=4,'mp'=4] {'dp'}, dimensions={0}, use_global_device_ids=true | all-gather | bytes 655360 | tf_op jit(solution)/shard_map/all_gather | solution.py:371
  262.8 0.0 all-reduce.2.cloned.1.call-done
  262.8 1.6 fusion.2
  264.4 0.1 reshape.17
  264.5 0.0 copy-done.1
  264.5 2.0 fusion
  266.5 0.1 reshape.19
  266.6 0.5 fusion.4
  267.1 6.2 %psum.15 = f32[4,32]{1,0:T(4,128)} all-reduce(f32[4,32]{1,0:T(4,128)S(1)} %fusion.4), channel_id=1, replica_groups=mesh['groups'=2,'dp'=4,'mp'=4] {'mp'}, use_global_device_ids=true, to_apply=%region_1.0 | all-reduce | flops 128 | bytes 1024 | tf_op jit(solution)/shard_map/psum | solution.py:399
  (1 shorter events, 0.0 us)
Async XLA Ops:
  6.5 2.5 copy-start
  6.5 2.5 copy-start.4
  6.5 256.3 %all-reduce.2.cloned.1.call-start = ((), (), s32[]{:S(2)}) async-start(), calls=%async_computation | async-start | bytes 1048576 | tf_op jit(solution)/shard_map/psum | solution.py:372
  19.1 8.5 %copy-start.2 = (bf16[2752,64]{0,1:T(8,128)(2,1)S(1)}, bf16[2752,64]{0,1:T(8,128)(2,1)}, u32[]{:S(2)}) copy-start(bf16[2752,64]{0,1:T(8,128)(2,1)} %param.16) | copy-start | bytes 1056772
  19.1 9.6 %copy-start.3 = (bf16[2752,64]{0,1:T(8,128)(2,1)S(1)}, bf16[2752,64]{0,1:T(8,128)(2,1)}, u32[]{:S(2)}) copy-start(bf16[2752,64]{0,1:T(8,128)(2,1)} %param.17) | copy-start | bytes 1056772
  29.8 212.0 %copy-start.5 = (bf16[8,8192]{1,0:T(8,128)(2,1)S(1)}, bf16[8,8192]{1,0:T(8,128)(2,1)}, u32[]{:S(2)}) copy-start(bf16[8,8192]{1,0:T(8,128)(2,1)} %param.19) | copy-start | bytes 393220
  241.8 22.7 %copy-start.1 = (f32[1024,64]{1,0:T(8,128)S(1)}, f32[1024,64]{1,0:T(8,128)}, u32[]{:S(2)}) copy-start(f32[1024,64]{1,0:T(8,128)} %get-tuple-element.8) | copy-start | bytes 786436
Sparse Core Ops, SparseCore 0:
  10.8 36.5 all-reduce.1

commit v2 on v1

--- a/solution.py
+++ b/solution.py
@@ -8,16 +8,19 @@
 from jax.sharding import PartitionSpec as P
 
 SEQ = 256
-PIECES = 4
+SHARES = (16, 36, 46, 40, 22, 12)
 MESH = pl.DeviceIdType.MESH
 NT = (((1,), (1,)), ((), ()))
-
-
-def cuts(total, parts):
-    units = -(-total // 128)
-    parts = min(parts, units)
-    edges = [min(total, 128 * ((units * i + parts - 1) // parts)) for i in range(parts + 1)]
-    return [(a, b - a) for a, b in zip(edges[:-1], edges[1:])]
+TN = (((0,), (0,)), ((), ()))
+
+
+def cuts(total):
+    units, whole, seen, edges = total // 16, sum(SHARES), 0, [0]
+    for share in SHARES:
+        seen += share
+        edges.append(16 * (units * seen // whole))
+    edges[-1] = total
+    return [(a, b - a) for a, b in zip(edges[:-1], edges[1:]) if b > a]
 
 
 def kernel(
@@ -28,8 +31,10 @@
     up_ref,
     up_out_ref,
     down_in_ref,
+    q_ref,
     out_up_ref,
     in_down_ref,
+    all_q_ref,
     wbuf,
     gbuf,
     gate,
@@ -45,24 +50,33 @@
     g_recv,
     r_send,
     r_recv,
+    q_send,
+    q_recv,
+    s_send,
+    s_recv,
 ):
     groups, dp, mp = sizes
-    tokens = gate.shape[0]
+    tokens = gate.shape[1]
     hidden_units, width = w_ref.shape
     half = width // groups
     gwidth = grad_ref.shape[1]
-    pieces = cuts(hidden_units, PIECES)
+    pieces = cuts(hidden_units)
     last = len(pieces) - 1
     y, z, m = (lax.axis_index(name) for name in ("groups", "dp", "mp"))
     x_count = mp // 2
     sibling = m + 1 - 2 * lax.rem(m, 2)
     has_lo, has_hi = z > 0, z < dp - 1
     tile = min(256, tokens)
-    small = min(128, tokens)
 
     def x_peer(j):
         return lax.rem(m + 2 * j, mp)
 
+    def m_peer(j):
+        return lax.rem(m + j, mp)
+
+    def z_peer(j):
+        return lax.rem(z + j, dp)
+
     def y_peer(j):
         return lax.rem(y + j, groups)
 
@@ -71,17 +85,13 @@
     def greet(where):
         pl.semaphore_signal(barrier, inc=1, device_id=where, device_id_type=MESH)
 
-    pl.when(has_lo)(lambda: greet({"dp": z - 1}))
-    pl.when(has_hi)(lambda: greet({"dp": z + 1}))
+    for j in range(1, dp):
+        greet({"dp": z_peer(j)})
     for j in range(1, groups):
         greet({"groups": y_peer(j)})
-    greet({"mp": sibling})
-    for j in range(1, x_count):
-        greet({"mp": x_peer(j)})
-    pl.semaphore_wait(
-        barrier,
-        has_lo.astype(jnp.int32) + has_hi.astype(jnp.int32) + (groups - 1) + 1 + (x_count - 1),
-    )
+    for j in range(1, mp):
+        greet({"mp": m_peer(j)})
+    pl.semaphore_wait(barrier, (dp - 1) + (groups - 1) + (mp - 1))
 
     def w_slice(ref, c, part):
         start, size = pieces[c]
@@ -149,6 +159,38 @@
         owner = lax.rem(m + mp - 2 * j, mp)
         return g_copy(sibling, owner, g_slice(gbuf, owner), r_send.at[j - 1], r_recv.at[j - 1])
 
+    def q_first(j):
+        return pltpu.make_async_remote_copy(
+            src_ref=q_ref,
+            dst_ref=all_q_ref.at[m, z],
+            send_sem=q_send.at[j - 1],
+            recv_sem=q_recv.at[j - 1],
+            device_id={"dp": z_peer(j)},
+            device_id_type=MESH,
+        )
+
+    def q_arrived(j):
+        pltpu.make_async_remote_copy(
+            src_ref=q_ref,
+            dst_ref=all_q_ref.at[m, lax.rem(z + dp - j, dp)],
+            send_sem=q_send.at[j - 1],
+            recv_sem=q_recv.at[j - 1],
+            device_id={"dp": z_peer(j)},
+            device_id_type=MESH,
+        ).wait_recv()
+
+    def q_second(j, owner):
+        return pltpu.make_async_remote_copy(
+            src_ref=all_q_ref.at[owner],
+            dst_ref=all_q_ref.at[owner],
+            send_sem=s_send.at[j - 1],
+            recv_sem=s_recv.at[j - 1],
+            device_id={"mp": m_peer(j)},
+            device_id_type=MESH,
+        )
+
+    for j in range(1, dp):
+        q_first(j).start()
     for c in range(len(pieces)):
         for way in (0, 1):
             pl.when(can_pass(way))(lambda way=way, c=c: z_copy(way, 0, c).start())
@@ -162,50 +204,61 @@
     w_in.start()
     g_in = pltpu.make_async_copy(grad_ref, g_slice(gbuf, m), local_sem.at[2])
     g_in.start()
+    q_in = pltpu.make_async_copy(q_ref, all_q_ref.at[m, z], local_sem.at[3])
+    q_in.start()
     gate_in.wait()
     w_in.wait()
     g_in.wait()
-
-    def silu(rows, start, size):
-        value = gate[rows, start : start + size].astype(jnp.float32)
+    q_in.wait()
+
+    def silu(rows, columns):
+        value = gate[rows, columns].astype(jnp.float32)
         return value / (1.0 + jnp.exp(-value))
 
-    def down_part(i):
-        base = i * tile
-        copy = pltpu.make_async_copy(up_ref.at[pl.ds(base, tile), :], upbuf, up_sem)
+    def columns_of(t):
+        return pl.ds(pl.multiple_of(t * tile, tile), tile)
+
+    def down_part(c):
+        start, size = pieces[c]
+        copy = pltpu.make_async_copy(
+            up_ref.at[pl.ds(start, size), :], upbuf.at[pl.ds(0, size), :], up_sem
+        )
         copy.start()
         copy.wait()
 
         def step(t, _):
-            inner = pl.ds(pl.multiple_of(t * small, small), small)
-            rows = pl.ds(pl.multiple_of(base + t * small, small), small)
-            total = jnp.zeros((small, in_down_ref.shape[1]), jnp.float32)
-            for start, size in pieces:
-                up = upbuf[inner, start : start + size].astype(jnp.float32)
-                hidden = (silu(rows, start, size) * up).astype(jnp.bfloat16)
-                total += jnp.dot(
-                    hidden, down_in_ref[start : start + size, :], preferred_element_type=jnp.float32
-                )
-            in_down_ref[rows, :] = total
+            columns = columns_of(t)
+            up = upbuf[0:size, columns].astype(jnp.float32)
+            hidden = (silu(pl.ds(start, size), columns) * up).astype(jnp.bfloat16)
+            share = lax.dot_general(
+                down_in_ref[start : start + size, :],
+                hidden,
+                TN,
+                preferred_element_type=jnp.float32,
+            )
+            if c == 0:
+                in_down_ref[:, columns] = share
+            else:
+                in_down_ref[:, columns] += share
             return 0
 
-        lax.fori_loop(0, tile // small, step, 0)
+        lax.fori_loop(0, tokens // tile, step, 0)
 
     def multiply(block, c, first):
         start, size = pieces[c]
 
         def step(t, _):
-            rows = pl.ds(pl.multiple_of(t * tile, tile), tile)
+            columns = columns_of(t)
             product = lax.dot_general(
-                gbuf[rows, pl.ds(pl.multiple_of(block * width, 128), width)],
                 wbuf[block, start : start + size, :],
+                gbuf[columns, pl.ds(pl.multiple_of(block * width, 128), width)],
                 NT,
                 preferred_element_type=jnp.float32,
             )
             if first:
-                acc[rows, start : start + size] = product
+                acc[start : start + size, columns] = product
             else:
-                acc[rows, start : start + size] += product
+                acc[start : start + size, columns] += product
             return 0
 
         lax.fori_loop(0, tokens // tile, step, 0)
@@ -214,18 +267,21 @@
         start, size = pieces[c]
 
         def step(t, _):
-            rows = pl.ds(pl.multiple_of(t * small, small), small)
-            up_grad = (acc[rows, start : start + size] * silu(rows, start, size)).astype(jnp.bfloat16)
-            share = jnp.dot(
-                up_grad, up_out_ref[start : start + size, :], preferred_element_type=jnp.float32
+            columns = columns_of(t)
+            up_grad = acc[start : start + size, columns] * silu(pl.ds(start, size), columns)
+            share = lax.dot_general(
+                up_out_ref[start : start + size, :],
+                up_grad.astype(jnp.bfloat16),
+                TN,
+                preferred_element_type=jnp.float32,
             )
             if c == 0:
-                out_up_ref[rows, :] = share
+                out_up_ref[:, columns] = share
             else:
-                out_up_ref[rows, :] += share
+                out_up_ref[:, columns] += share
             return 0
 
-        lax.fori_loop(0, tokens // small, step, 0)
+        lax.fori_loop(0, tokens // tile, step, 0)
 
     def consume(k, c):
         if k == 0:
@@ -248,7 +304,7 @@
         for j in range(1, x_count):
             g_relay(j).wait_recv()
 
-    down_todo = list(range(tokens // tile))
+    down_todo = list(range(len(pieces)))
     todo = [(0, c) for c in range(len(pieces))]
     ready = False
     for k in range(1, dp):
@@ -266,6 +322,11 @@
             if k == 1:
                 if down_todo:
                     down_part(down_todo.pop(0))
+                if c == 1:
+                    for j in range(1, dp):
+                        q_arrived(j)
+                    for j in range(1, mp):
+                        q_second(j, m).start()
                 if c == last:
                     for j in range(1, x_count):
                         g_first(j).wait_recv()
@@ -274,9 +335,9 @@
                 if not ready:
                     gather_grad()
                     ready = True
-                for item in todo[:3]:
+                for item in todo[:2]:
                     consume(*item)
-                todo = todo[3:]
+                todo = todo[2:]
             todo.append((k, c))
     if not ready:
         gather_grad()
@@ -285,6 +346,13 @@
     for item in todo:
         consume(*item)
 
+    for j in range(1, mp):
+        q_second(j, lax.rem(m + mp - j, mp)).wait_recv()
+
+    for j in range(1, dp):
+        q_first(j).wait_send()
+    for j in range(1, mp):
+        q_second(j, m).wait_send()
     for k in range(dp):
         for way in (0, 1):
             for c in range(len(pieces)):
@@ -304,30 +372,30 @@
         g_relay(j).wait_send()
 
 
-def gather_and_project(sizes, down_weight, output_grad, gate, up, up_out, down_in):
+def gather_and_project(sizes, down_weight, output_grad, gate, up, up_out, down_in, own_queries):
     groups, dp, mp = sizes
-    tokens, hidden_units = gate.shape
+    hidden_units, tokens = gate.shape
     rank = up_out.shape[1]
     width = down_weight.shape[1]
-    count = len(cuts(hidden_units, PIECES))
+    pieces = cuts(hidden_units)
+    count = len(pieces)
     x_count = mp // 2
-    tile = min(256, tokens)
     anywhere = pl.BlockSpec(memory_space=pl.ANY)
     vmem = pl.BlockSpec(memory_space=pltpu.VMEM)
     dma = pltpu.SemaphoreType.DMA
-    part = jax.ShapeDtypeStruct((tokens, rank), jnp.float32)
+    part = jax.ShapeDtypeStruct((rank, tokens), jnp.float32)
     return pl.pallas_call(
         functools.partial(kernel, sizes),
-        out_shape=(part, part),
-        in_specs=[anywhere] * 4 + [vmem] * 2,
-        out_specs=(vmem, vmem),
+        out_shape=(part, part, jax.ShapeDtypeStruct((mp, dp) + own_queries.shape, jnp.bfloat16)),
+        in_specs=[anywhere] * 4 + [vmem] * 3,
+        out_specs=(vmem, vmem, vmem),
         scratch_shapes=[
             pltpu.VMEM((dp, hidden_units, width), jnp.bfloat16),
             pltpu.VMEM((tokens, output_grad.shape[1] * mp), jnp.bfloat16),
-            pltpu.VMEM((tokens, hidden_units), jnp.bfloat16),
-            pltpu.VMEM((tile, hidden_units), jnp.bfloat16),
-            pltpu.VMEM((tokens, hidden_units), jnp.float32),
-            dma((3,)),
+            pltpu.VMEM((hidden_units, tokens), jnp.bfloat16),
+            pltpu.VMEM((max(size for _, size in pieces), tokens), jnp.bfloat16),
+            pltpu.VMEM((hidden_units, tokens), jnp.float32),
+            dma((4,)),
             dma,
             dma((2, dp, count)),
             dma((dp, count)),
@@ -337,6 +405,10 @@
             dma((x_count,)),
             dma((max(x_count - 1, 1),)),
             dma((max(x_count - 1, 1),)),
+            dma((max(dp - 1, 1),)),
+            dma((max(dp - 1, 1),)),
+            dma((max(mp - 1, 1),)),
+            dma((max(mp - 1, 1),)),
         ],
         compiler_params=pltpu.CompilerParams(
             collective_id=0, has_side_effects=True, vmem_limit_bytes=60 * 1024 * 1024
@@ -346,7 +418,7 @@
             bytes_accessed=4 * tokens * hidden_units,
             transcendentals=2 * tokens * hidden_units,
         ),
-    )(down_weight, output_grad, gate, up, up_out, down_in)
+    )(down_weight, output_grad, gate, up, up_out, down_in, own_queries)
 
 
 def outer_sums(first, second):
@@ -366,9 +438,12 @@
     down_out_factor,
     queries,
 ):
+    groups, dp, mp = sizes
     rank = up_in_factor.shape[1]
     count = output_grad.shape[0] // SEQ
-    all_queries = lax.all_gather(queries, "dp", axis=0, tiled=True)
+    query_rows, sketch_size = queries.shape
+    share = sketch_size // mp
+    own_queries = lax.dynamic_slice_in_dim(queries, lax.axis_index("mp") * share, share, 1)
     early = lax.psum(
         jnp.concatenate(
             [
@@ -379,23 +454,39 @@
         ),
         "mp",
     ).reshape(count, SEQ, 2 * rank)
-    out_up, in_down = gather_and_project(
-        sizes, down_weight, output_grad, gate_preact, up_values, up_out_factor, down_in_factor
+    out_up, in_down, all_queries = gather_and_project(
+        sizes,
+        down_weight,
+        output_grad,
+        gate_preact.T,
+        up_values.T,
+        up_out_factor,
+        down_in_factor,
+        own_queries.reshape(query_rows * share // 128, 128),
     )
     sketch = jnp.concatenate(
         [
-            outer_sums(early[:, :, :rank], out_up.reshape(count, SEQ, rank)).reshape(count, -1),
-            outer_sums(in_down.reshape(count, SEQ, rank), early[:, :, rank:]).reshape(count, -1),
+            jnp.einsum(
+                "nti,jnt->nij",
+                early[:, :, :rank],
+                out_up.reshape(rank, count, SEQ),
+                precision=lax.Precision.HIGHEST,
+            ).reshape(count, -1),
+            jnp.einsum(
+                "int,ntj->nij",
+                in_down.reshape(rank, count, SEQ),
+                early[:, :, rank:],
+                precision=lax.Precision.HIGHEST,
+            ).reshape(count, -1),
         ],
         1,
     )
-    scores = lax.dot_general(
-        sketch,
-        all_queries.astype(jnp.float32),
-        NT,
+    scores = jnp.einsum(
+        "nmc,mdqc->ndq",
+        sketch.reshape(count, mp, share),
+        all_queries.reshape(mp, dp, query_rows, share).astype(jnp.float32),
         precision=lax.Precision.HIGHEST,
-        preferred_element_type=jnp.float32,
-    )
+    ).reshape(count, dp * query_rows)
     return lax.psum(scores, "mp")
 
 

time: 281 us -> 247 us (0.88)
  blocking collectives: 27.2 us -> 6.22 us
  local copies, waits for them, and re-layouts: 20.1 us -> 7.75 us
    all_gather x1 -> x0, blocking collectives: 21 us -> none  [body(): all_queries = lax.all_gather(queries, 'dp', axis=0, tiled=True)]
    unnamed x16 -> x14, local copies, waits for them, and re-layouts: 19.1 us -> 3.89 us
  transfers between devices with their start and end apart: 1 -> 1, of which waited for: 0 -> 0; matrix products, arithmetic and copies ran while one was open for 7% -> 2% of each run, Pallas kernels for 76% -> 86%
where the time goes in v2:
time: 247 us
  Pallas kernels  213 us (86%)
  between operations  13.5 us (5%)
  local copies, waits for them, and re-layouts  7.75 us (3%)
  blocking collectives  6.22 us (3%)
  matrix products  5.84 us (2%)
    pallas_call x1, Pallas kernels, gather_and_project(): pl.pallas_call(functools.partial(kernel, sizes), out_shape=(part, part, j...  213 us
    psum x1, blocking collectives, body(): return lax.psum(scores, 'mp')  6.22 us
  transfers between devices with their start and end apart: 1, of which 0 were waited for; matrix products, arithmetic and copies ran while one was open for 2% of the time, Pallas kernels for 86%

profile of v2, /device:TPU:0, one launch (start us, length us, event | category | flops | bytes accessed | tf_op | source)
XLA Modules:
  0.0 246.7 jit_solution(1426247117601953719)
XLA Ops:
  6.5 0.0 copy-start
  6.5 0.0 copy-start.5
  6.5 0.0 all-reduce.2.cloned.1.call-start
  6.5 1.6 copy-done
  8.1 0.0 copy-start.1
  8.1 1.8 fusion.13
  9.9 0.0 copy-done.5
  9.9 0.0 copy-done.1
  10.0 0.0 copy-start.2
  10.0 0.8 fusion.14
  10.7 0.0 copy-start.3
  10.8 0.8 copy.30
  11.6 0.0 all-reduce.2.cloned.1.call-update
  11.7 0.8 constant_dynamic-slice_fusion
  12.4 0.6 reshape.25.q_ref
  13.0 0.0 copy-done.2
  13.1 1.1 copy.12.up_out_ref
  14.2 0.0 copy-done.3
  14.2 1.2 copy.13.down_in_ref
  15.3 213.3 %shard_map.100 = (f32[64,1024]{1,0:T(8,128)}, f32[64,1024]{1,0:T(8,128)}, bf16[4,4,128,128]{3,2,1,0:T(8,128)(2,1)}) custom-call(bf16[2752,1024]{1,0:T(8,128)(2,1)} %w_ref.1, bf16[1024,1024]{1,0:T(8,128)(2,1)} %grad_ref.1, bf16[2752,1024]{1,0:T(8,128)(2,1)} %bitcast.31, bf16[2752,1024]{1,0:T(8,128)(2,1)} %bitcast.32, bf16[2752,64]{1,0:T(8,128)(2,1)} %copy.12.up_out_ref, ...), custom_call_target="tpu_custom_call" | custom-call | flops 23085449216 | bytes 11272192 | tf_op jit(solution)/shard_map/pallas_call | solution.py:387
  228.6 0.0 copy-start.4
  228.7 1.3 reshape.28
  230.0 0.0 all-reduce.2.cloned.1.call-done
  230.0 1.4 fusion.4
  231.4 0.1 concatenate.12
  231.6 0.0 copy-done.4
  231.6 1.3 fusion.1
  232.9 0.1 concatenate.13
  233.1 0.5 convolution_bitcast_fusion
  233.6 6.2 %psum.15 = f32[4,32]{1,0:T(4,128)} all-reduce(f32[4,32]{1,0:T(4,128)S(1)} %convolution_bitcast_fusion), channel_id=1, replica_groups=mesh['groups'=2,'dp'=4,'mp'=4] {'mp'}, use_global_device_ids=true, to_apply=%region_1.0 | all-reduce | flops 128 | bytes 1024 | tf_op jit(solution)/shard_map/psum | solution.py:490
  (3 shorter events, 0.1 us)
Async XLA Ops:
  6.5 1.6 copy-start
  6.5 3.4 %copy-start.5 = (bf16[1024,64]{0,1:T(8,128)(2,1)S(1)}, bf16[1024,64]{0,1:T(8,128)(2,1)}, u32[]{:S(2)}) copy-start(bf16[1024,64]{0,1:T(8,128)(2,1)} %param.18) | copy-start | bytes 393220
  6.5 223.5 %all-reduce.2.cloned.1.call-start = ((), (), s32[]{:S(2)}) async-start(), calls=%async_computation | async-start | bytes 1048576 | tf_op jit(solution)/shard_map/psum | solution.py:447
  8.1 1.8 copy-start.1
  10.0 3.1 %copy-start.2 = (bf16[2752,64]{0,1:T(8,128)(2,1)S(1)}, bf16[2752,64]{0,1:T(8,128)(2,1)}, u32[]{:S(2)}) copy-start(bf16[2752,64]{0,1:T(8,128)(2,1)} %param.16) | copy-start | bytes 1056772
  10.7 3.5 %copy-start.3 = (bf16[2752,64]{0,1:T(8,128)(2,1)S(1)}, bf16[2752,64]{0,1:T(8,128)(2,1)}, u32[]{:S(2)}) copy-start(bf16[2752,64]{0,1:T(8,128)(2,1)} %param.17) | copy-start | bytes 1056772
  228.6 2.9 %copy-start.4 = (f32[64,1024]{1,0:T(8,128)S(1)}, f32[64,1024]{1,0:T(8,128)}, u32[]{:S(2)}) copy-start(f32[64,1024]{1,0:T(8,128)} %get-tuple-element.9) | copy-start | bytes 786436
Sparse Core Ops, SparseCore 0:
  11.8 40.4 all-reduce.1

commit v3 on v2

--- a/solution.py
+++ b/solution.py
@@ -8,18 +8,16 @@
 from jax.sharding import PartitionSpec as P
 
 SEQ = 256
-SHARES = (16, 36, 46, 40, 22, 12)
+SHARES = (2, 5, 6, 5, 2, 2)
 MESH = pl.DeviceIdType.MESH
 NT = (((1,), (1,)), ((), ()))
-TN = (((0,), (0,)), ((), ()))
 
 
 def cuts(total):
-    units, whole, seen, edges = total // 16, sum(SHARES), 0, [0]
+    units, whole, seen, edges = -(-total // 128), sum(SHARES), 0, [0]
     for share in SHARES:
         seen += share
-        edges.append(16 * (units * seen // whole))
-    edges[-1] = total
+        edges.append(min(total, 128 * (units * seen // whole)))
     return [(a, b - a) for a, b in zip(edges[:-1], edges[1:]) if b > a]
 
 
@@ -32,9 +30,16 @@
     up_out_ref,
     down_in_ref,
     q_ref,
+    layer_ref,
+    up_in_ref,
+    down_out_ref,
+    sketch_ref,
+    all_q_ref,
     out_up_ref,
     in_down_ref,
-    all_q_ref,
+    early,
+    parts,
+    summed,
     wbuf,
     gbuf,
     gate,
@@ -54,6 +59,10 @@
     q_recv,
     s_send,
     s_recv,
+    e_send,
+    e_recv,
+    t_send,
+    t_recv,
 ):
     groups, dp, mp = sizes
     tokens = gate.shape[1]
@@ -218,6 +227,69 @@
     def columns_of(t):
         return pl.ds(pl.multiple_of(t * tile, tile), tile)
 
+    rank = up_in_ref.shape[0]
+    share_rows = 2 * rank // mp
+
+    def early_rows(owner):
+        return pl.ds(pl.multiple_of(owner * share_rows, 8), share_rows)
+
+    def early_part():
+        room = min(tokens, upbuf.shape[0])
+        for first in range(0, tokens, room):
+            count = min(room, tokens - first)
+            copy = pltpu.make_async_copy(
+                layer_ref.at[pl.ds(first, count), :],
+                upbuf.at[pl.ds(0, count), pl.ds(0, gwidth)],
+                up_sem,
+            )
+            copy.start()
+            copy.wait()
+            early[0:rank, first : first + count] = lax.dot_general(
+                up_in_ref[...], upbuf[0:count, 0:gwidth], NT, preferred_element_type=jnp.float32
+            )
+
+        def step(t, _):
+            columns = columns_of(t)
+            early[rank : 2 * rank, columns] = lax.dot_general(
+                down_out_ref[...],
+                gbuf[columns, pl.ds(pl.multiple_of(m * gwidth, 128), gwidth)],
+                NT,
+                preferred_element_type=jnp.float32,
+            )
+            return 0
+
+        lax.fori_loop(0, tokens // tile, step, 0)
+
+    def early_out(j):
+        return pltpu.make_async_remote_copy(
+            src_ref=early.at[early_rows(m_peer(j))],
+            dst_ref=parts.at[j - 1],
+            send_sem=e_send.at[j - 1],
+            recv_sem=e_recv.at[j - 1],
+            device_id={"mp": m_peer(j)},
+            device_id_type=MESH,
+        )
+
+    def early_back(j, owner):
+        return pltpu.make_async_remote_copy(
+            src_ref=summed.at[early_rows(owner)],
+            dst_ref=summed.at[early_rows(owner)],
+            send_sem=t_send.at[j - 1],
+            recv_sem=t_recv.at[j - 1],
+            device_id={"mp": m_peer(j)},
+            device_id_type=MESH,
+        )
+
+    def early_sum():
+        rows = early_rows(m)
+        total = early[rows, :]
+        for j in range(1, mp):
+            early_out(j).wait_recv()
+            total += parts[j - 1]
+        summed[rows, :] = total
+        for j in range(1, mp):
+            early_back(j, m).start()
+
     def down_part(c):
         start, size = pieces[c]
         copy = pltpu.make_async_copy(
@@ -230,11 +302,8 @@
             columns = columns_of(t)
             up = upbuf[0:size, columns].astype(jnp.float32)
             hidden = (silu(pl.ds(start, size), columns) * up).astype(jnp.bfloat16)
-            share = lax.dot_general(
-                down_in_ref[start : start + size, :],
-                hidden,
-                TN,
-                preferred_element_type=jnp.float32,
+            share = jnp.dot(
+                down_in_ref[:, start : start + size], hidden, preferred_element_type=jnp.float32
             )
             if c == 0:
                 in_down_ref[:, columns] = share
@@ -269,10 +338,9 @@
         def step(t, _):
             columns = columns_of(t)
             up_grad = acc[start : start + size, columns] * silu(pl.ds(start, size), columns)
-            share = lax.dot_general(
-                up_out_ref[start : start + size, :],
+            share = jnp.dot(
+                up_out_ref[:, start : start + size],
                 up_grad.astype(jnp.bfloat16),
-                TN,
                 preferred_element_type=jnp.float32,
             )
             if c == 0:
@@ -322,6 +390,12 @@
             if k == 1:
                 if down_todo:
                     down_part(down_todo.pop(0))
+                if c == 0:
+                    early_part()
+                    for j in range(1, mp):
+                        early_out(j).start()
+                if c == 2:
+                    early_sum()
                 if c == 1:
                     for j in range(1, dp):
                         q_arrived(j)
@@ -349,6 +423,28 @@
     for j in range(1, mp):
         q_second(j, lax.rem(m + mp - j, mp)).wait_recv()
 
+    for j in range(1, mp):
+        early_back(j, lax.rem(m + mp - j, mp)).wait_recv()
+
+    for n in range(tokens // SEQ):
+        own = pl.ds(n * SEQ, SEQ)
+        for part, (first, second) in enumerate(
+            (
+                (summed[0:rank, own], out_up_ref[:, own]),
+                (in_down_ref[:, own], summed[rank : 2 * rank, own]),
+            )
+        ):
+            sketch_ref[n, part * rank : (part + 1) * rank, :] = lax.dot_general(
+                first,
+                second,
+                NT,
+                precision=lax.Precision.HIGHEST,
+                preferred_element_type=jnp.float32,
+            )
+
+    for j in range(1, mp):
+        early_out(j).wait_send()
+        early_back(j, m).wait_send()
     for j in range(1, dp):
         q_first(j).wait_send()
     for j in range(1, mp):
@@ -372,10 +468,22 @@
         g_relay(j).wait_send()
 
 
-def gather_and_project(sizes, down_weight, output_grad, gate, up, up_out, down_in, own_queries):
+def gather_and_project(
+    sizes,
+    down_weight,
+    output_grad,
+    gate,
+    up,
+    up_out,
+    down_in,
+    own_queries,
+    layer_input,
+    up_in,
+    down_out,
+):
     groups, dp, mp = sizes
     hidden_units, tokens = gate.shape
-    rank = up_out.shape[1]
+    rank = up_out.shape[0]
     width = down_weight.shape[1]
     pieces = cuts(hidden_units)
     count = len(pieces)
@@ -383,17 +491,25 @@
     anywhere = pl.BlockSpec(memory_space=pl.ANY)
     vmem = pl.BlockSpec(memory_space=pltpu.VMEM)
     dma = pltpu.SemaphoreType.DMA
-    part = jax.ShapeDtypeStruct((rank, tokens), jnp.float32)
+    gwidth = output_grad.shape[1]
     return pl.pallas_call(
         functools.partial(kernel, sizes),
-        out_shape=(part, part, jax.ShapeDtypeStruct((mp, dp) + own_queries.shape, jnp.bfloat16)),
-        in_specs=[anywhere] * 4 + [vmem] * 3,
-        out_specs=(vmem, vmem, vmem),
+        out_shape=(
+            jax.ShapeDtypeStruct((tokens // SEQ, 2 * rank, rank), jnp.float32),
+            jax.ShapeDtypeStruct((mp, dp) + own_queries.shape, jnp.bfloat16),
+        ),
+        in_specs=[anywhere] * 4 + [vmem] * 3 + [anywhere] + [vmem] * 2,
+        out_specs=(vmem, vmem),
         scratch_shapes=[
+            pltpu.VMEM((rank, tokens), jnp.float32),
+            pltpu.VMEM((rank, tokens), jnp.float32),
+            pltpu.VMEM((2 * rank, tokens), jnp.float32),
+            pltpu.VMEM((max(mp - 1, 1), 2 * rank // mp, tokens), jnp.float32),
+            pltpu.VMEM((2 * rank, tokens), jnp.float32),
             pltpu.VMEM((dp, hidden_units, width), jnp.bfloat16),
             pltpu.VMEM((tokens, output_grad.shape[1] * mp), jnp.bfloat16),
             pltpu.VMEM((hidden_units, tokens), jnp.bfloat16),
-            pltpu.VMEM((max(size for _, size in pieces), tokens), jnp.bfloat16),
+            pltpu.VMEM((max(size for _, size in pieces), max(tokens, gwidth)), jnp.bfloat16),
             pltpu.VMEM((hidden_units, tokens), jnp.float32),
             dma((4,)),
             dma,
@@ -407,9 +523,8 @@
             dma((max(x_count - 1, 1),)),
             dma((max(dp - 1, 1),)),
             dma((max(dp - 1, 1),)),
-            dma((max(mp - 1, 1),)),
-            dma((max(mp - 1, 1),)),
-        ],
+        ]
+        + [dma((max(mp - 1, 1),))] * 6,
         compiler_params=pltpu.CompilerParams(
             collective_id=0, has_side_effects=True, vmem_limit_bytes=60 * 1024 * 1024
         ),
@@ -418,11 +533,18 @@
             bytes_accessed=4 * tokens * hidden_units,
             transcendentals=2 * tokens * hidden_units,
         ),
-    )(down_weight, output_grad, gate, up, up_out, down_in, own_queries)
-
-
-def outer_sums(first, second):
-    return jnp.einsum("nti,ntj->nij", first, second, precision=lax.Precision.HIGHEST)
+    )(
+        down_weight,
+        output_grad,
+        gate,
+        up,
+        up_out,
+        down_in,
+        own_queries,
+        layer_input,
+        up_in,
+        down_out,
+    )
 
 
 def body(
@@ -439,47 +561,22 @@
     queries,
 ):
     groups, dp, mp = sizes
-    rank = up_in_factor.shape[1]
     count = output_grad.shape[0] // SEQ
     query_rows, sketch_size = queries.shape
     share = sketch_size // mp
     own_queries = lax.dynamic_slice_in_dim(queries, lax.axis_index("mp") * share, share, 1)
-    early = lax.psum(
-        jnp.concatenate(
-            [
-                jnp.dot(layer_input, up_in_factor, preferred_element_type=jnp.float32),
-                jnp.dot(output_grad, down_out_factor, preferred_element_type=jnp.float32),
-            ],
-            1,
-        ),
-        "mp",
-    ).reshape(count, SEQ, 2 * rank)
-    out_up, in_down, all_queries = gather_and_project(
+    sketch, all_queries = gather_and_project(
         sizes,
         down_weight,
         output_grad,
         gate_preact.T,
         up_values.T,
-        up_out_factor,
-        down_in_factor,
+        up_out_factor.T,
+        down_in_factor.T,
         own_queries.reshape(query_rows * share // 128, 128),
-    )
-    sketch = jnp.concatenate(
-        [
-            jnp.einsum(
-                "nti,jnt->nij",
-                early[:, :, :rank],
-                out_up.reshape(rank, count, SEQ),
-                precision=lax.Precision.HIGHEST,
-            ).reshape(count, -1),
-            jnp.einsum(
-                "int,ntj->nij",
-                in_down.reshape(rank, count, SEQ),
-                early[:, :, rank:],
-                precision=lax.Precision.HIGHEST,
-            ).reshape(count, -1),
-        ],
-        1,
+        layer_input,
+        up_in_factor.T,
+        down_out_factor.T,
     )
     scores = jnp.einsum(
         "nmc,mdqc->ndq",

time: 247 us -> 225 us (0.911)
  between operations: 13.5 us -> 0.02 us
  matrix products: 5.84 us -> 0.6 us
  local copies, waits for them, and re-layouts: 7.75 us -> 3.88 us
    dot_general x4 -> x0, matrix products: 5.31 us -> none  [the longest x1 1.81 us: body(): jnp.dot(layer_input, up_in_factor, preferred_element_type=jnp.float32)]
    unnamed x14 -> x2, local copies, waits for them, and re-layouts: 3.89 us -> 0.9 us
  transfers between devices with their start and end apart: 1 -> 0, of which waited for: 0 -> 0; matrix products, arithmetic and copies ran while one was open for 2% -> 0% of each run, Pallas kernels for 86% -> 0%
where the time goes in v3:
time: 225 us
  Pallas kernels  214 us (95%)
  blocking collectives  6.22 us (3%)
  local copies, waits for them, and re-layouts  3.88 us (2%)
    pallas_call x1, Pallas kernels, gather_and_project(): pl.pallas_call(functools.partial(kernel, sizes), out_shape=(jax.ShapeDtyp...  214 us
    psum x1, blocking collectives, body(): return lax.psum(scores, 'mp')  6.22 us

profile of v3, /device:TPU:0, one launch (start us, length us, event | category | flops | bytes accessed | tf_op | source)
XLA Modules:
  0.0 224.8 jit_solution(8582907309270793747)
XLA Ops:
  0.0 0.0 copy-start
  0.0 0.9 copy-done
  0.9 0.6 reshape.11.q_ref
  1.5 214.1 %shard_map.100 = (f32[4,128,64]{2,1,0:T(8,128)}, bf16[4,4,128,128]{3,2,1,0:T(8,128)(2,1)}) custom-call(bf16[2752,1024]{1,0:T(8,128)(2,1)} %w_ref.1, bf16[1024,1024]{1,0:T(8,128)(2,1)} %grad_ref.1, bf16[2752,1024]{1,0:T(8,128)(2,1)} %bitcast.15, bf16[2752,1024]{1,0:T(8,128)(2,1)} %bitcast.16, bf16[64,2752]{1,0:T(8,128)(2,1)} %bitcast.17, ...), custom_call_target="tpu_custom_call" | custom-call | flops 23085449216 | bytes 11272192 | tf_op jit(solution)/shard_map/pallas_call | solution.py:495
  215.7 1.1 reshape.12
  216.8 1.3 reshape.13
  218.0 0.6 convolution_bitcast_fusion
  218.6 6.2 %psum.7 = f32[4,32]{1,0:T(4,128)} all-reduce(f32[4,32]{1,0:T(4,128)S(1)} %convolution_bitcast_fusion), channel_id=1, replica_groups=mesh['groups'=2,'dp'=4,'mp'=4] {'mp'}, use_global_device_ids=true, to_apply=%region_0.0 | all-reduce | flops 128 | bytes 1024 | tf_op jit(solution)/shard_map/psum | solution.py:587
  (1 shorter events, 0.0 us)
Async XLA Ops:
  0.0 0.9 copy-start

commit v4 on v3

--- a/solution.py
+++ b/solution.py
@@ -8,7 +8,7 @@
 from jax.sharding import PartitionSpec as P
 
 SEQ = 256
-SHARES = (2, 5, 6, 5, 2, 2)
+SHARES = (1, 4, 6, 6, 4, 1)
 MESH = pl.DeviceIdType.MESH
 NT = (((1,), (1,)), ((), ()))
 

time: 225 us -> 230 us (1.022)
  Pallas kernels: 214 us -> 218 us
    pallas_call x1, Pallas kernels: 214 us -> 218 us  [gather_and_project(): pl.pallas_call(functools.partial(kernel, sizes), out_shape=(jax.ShapeDtyp...]
where the time goes in v4:
time: 230 us; the launch traced here: 229 us
  Pallas kernels  218 us (95%)
  blocking collectives  7.08 us (3%)
  local copies, waits for them, and re-layouts  3.88 us (2%)
    pallas_call x1, Pallas kernels, gather_and_project(): pl.pallas_call(functools.partial(kernel, sizes), out_shape=(jax.ShapeDtyp...  218 us
    psum x1, blocking collectives, body(): return lax.psum(scores, 'mp')  7.08 us

profile of v4, /device:TPU:0, one launch (start us, length us, event | category | flops | bytes accessed | tf_op | source)
XLA Modules:
  0.0 229.2 jit_solution(12618803839753566610)
XLA Ops:
  0.0 0.0 copy-start
  0.0 0.9 copy-done
  0.9 0.6 reshape.11.q_ref
  1.5 217.7 %shard_map.100 = (f32[4,128,64]{2,1,0:T(8,128)}, bf16[4,4,128,128]{3,2,1,0:T(8,128)(2,1)}) custom-call(bf16[2752,1024]{1,0:T(8,128)(2,1)} %w_ref.1, bf16[1024,1024]{1,0:T(8,128)(2,1)} %grad_ref.1, bf16[2752,1024]{1,0:T(8,128)(2,1)} %bitcast.15, bf16[2752,1024]{1,0:T(8,128)(2,1)} %bitcast.16, bf16[64,2752]{1,0:T(8,128)(2,1)} %bitcast.17, ...), custom_call_target="tpu_custom_call" | custom-call | flops 23085449216 | bytes 11272192 | tf_op jit(solution)/shard_map/pallas_call | solution.py:495
  219.2 1.1 reshape.12
  220.3 1.3 reshape.13
  221.6 0.6 convolution_bitcast_fusion
  222.2 7.1 %psum.7 = f32[4,32]{1,0:T(4,128)} all-reduce(f32[4,32]{1,0:T(4,128)S(1)} %convolution_bitcast_fusion), channel_id=1, replica_groups=mesh['groups'=2,'dp'=4,'mp'=4] {'mp'}, use_global_device_ids=true, to_apply=%region_0.0 | all-reduce | flops 128 | bytes 1024 | tf_op jit(solution)/shard_map/psum | solution.py:587
  (1 shorter events, 0.0 us)
Async XLA Ops:
  0.0 0.9 copy-start
